TPU v7x, 32 devices: a whole 2x2x4 slice. The times are simulated.
32 devices in a mesh: template: 4 (over y, core), fsdp: 4 (over z), dp: 2 (over x).
Axes of the slice: x: 2, y: 2, z: 4, core: 2. Of those that a mesh axis runs over, the one named last changes fastest.
Arguments:
- hidden: bfloat16 [4, 1024, 8192], P('template', ('fsdp', 'dp')), may hold values from -6 to 6
- target: bfloat16 [4, 1024, 512], P('template', ('fsdp', 'dp')), may hold values from -6 to 6
- weight: bfloat16 [4, 8192, 512], P('template', 'fsdp'), may hold values from -6 to 6
- gain: bfloat16 [4, 8192], P('template', 'fsdp'), may hold values from 0.099609375 to 1.8984375
Outputs:
- merged_weight: float32 [8192, 512], P(('fsdp', 'dp'))
- merged_gain: float32 [8192], P(('fsdp', 'dp'))
All inputs are finite; a program needn't handle non-finite values.
Results may differ from a plain program's by a relative error of at most 0.0018.
Values may be sent and summed in bfloat16 or wider, within the bound.
A program may use at most 64 MiB of HBM per device.

v0:
```python
import math

import jax
import jax.numpy as jnp
from jax import lax
from jax.sharding import PartitionSpec as P


def body(hidden, target, weight, gain):
    token_batch = hidden[0]
    goal = target[0]
    w_shard = weight[0]
    g_shard = gain[0]
    width = token_batch.shape[1]
    scale = 1.0 / math.sqrt(width)
    merge_quotient = lax.rsqrt(
        jnp.mean(jnp.square(token_batch.astype(jnp.float32)), axis=1, keepdims=True) + 1e-05
    )
    w_full, complete_gain = (
        lax.all_gather(w_shard, "fsdp", axis=0, tiled=True),
        lax.all_gather(g_shard, "fsdp", axis=0, tiled=True),
    )
    normalized_activation = token_batch.astype(jnp.float32) * merge_quotient
    normalized_input = (normalized_activation * complete_gain.astype(jnp.float32)[None, :]).astype(
        jnp.bfloat16
    )
    values = jnp.dot(normalized_input, w_full, preferred_element_type=jnp.float32) * scale
    delta = (values - goal.astype(jnp.float32)).astype(jnp.bfloat16)
    backward_pass = (
        jnp.einsum("th,dh->td", delta, w_full, preferred_element_type=jnp.float32) * scale
    )
    gain_information = jnp.sum(jnp.square(backward_pass * normalized_activation), axis=0)
    sq_normed = jnp.square(normalized_input.astype(jnp.float32)).astype(jnp.bfloat16)
    sq_delta = jnp.square(delta.astype(jnp.float32)).astype(jnp.bfloat16)
    mine = width // lax.axis_size(("fsdp", "dp"))
    columns = lax.all_to_all(sq_normed, ("fsdp", "dp"), split_axis=1, concat_axis=0, tiled=True)
    fisher = jnp.einsum(
        "td,th->dh",
        columns,
        lax.all_gather(sq_delta, ("fsdp", "dp"), axis=0, tiled=True),
        preferred_element_type=jnp.float32,
    )
    gain_total = lax.psum(gain_information.astype(jnp.bfloat16), ("fsdp", "dp")).astype(jnp.float32)
    where = lax.axis_index(("fsdp", "dp")) * mine
    gain_information_sum = lax.dynamic_slice_in_dim(gain_total, where, mine, 0)
    offset = lax.axis_index("dp") * mine
    theta = lax.dynamic_slice_in_dim(w_shard, offset, mine, 0).astype(jnp.float32)
    gmine = lax.dynamic_slice_in_dim(g_shard, offset, mine, 0).astype(jnp.float32)
    weighted = fisher * theta
    gain_weighted = (gain_information_sum * gmine)[:, None]
    gain_column = gain_information_sum[:, None]
    num, den, gnum, gden = lax.psum((weighted, fisher, gain_weighted, gain_column), "template")
    return (num / den, gnum[:, 0] / gden[:, 0])


def solution(mesh):
    in_specs = (
        P("template", ("fsdp", "dp"), None),
        P("template", ("fsdp", "dp"), None),
        P("template", "fsdp", None),
        P("template", "fsdp"),
    )
    out_specs = (P(("fsdp", "dp"), None), P(("fsdp", "dp")))
    return jax.shard_map(body, mesh=mesh, in_specs=in_specs, out_specs=out_specs, check_vma=False)
```

profile of v0, /device:TPU:1, one launch (start us, length us, event | category | flops | bytes accessed | tf_op | source)
XLA Modules:
  0.0 350.4 jit_solution(13375214823142482440)
XLA Ops:
  7.2 0.0 copy-start
  7.2 0.0 all-gather.7.cloned.1.call-start
  7.2 0.7 all-gather.7.cloned.1.call-update
  7.9 11.8 %all-gather = bf16[1,8192]{1,0:T(2,128)(2,1)S(1)} all-gather(bf16[1,2048]{1,0:T(2,128)(2,1)} %param.7), channel_id=2, replica_groups=mesh['template'=4,'fsdp'=4,'dp'=2] {'fsdp'}, dimensions={1}, use_global_device_ids=true | all-gather | bytes 20480 | tf_op jit(solution)/shard_map/all_gather | solution.py:21
  19.7 0.1 convert_reduce_fusion
  19.8 3.6 %copy.7 = f32[16,8,8,1024]{3,2,1,0:T(8,128)S(1)} copy(bf16[16,8,8,1024]{3,1,2,0:T(8,128)(2,1)} %bitcast.58) | data formatting | bytes 6291456
  23.4 0.0 copy-done
  23.4 0.5 fusion.5
  23.9 0.0 copy-start.3
  23.9 3.8 %multiply_convert_fusion.1 = bf16[128,8,1024]{2,0,1:T(8,128)(2,1)} fusion(f32[128,8,1024]{2,1,0:T(8,128)S(1)} %bitcast.56, f32[8,1024]{1,0:T(8,128)S(1)} %mul.60, f32[128]{0:T(128)S(1)} %add_rsqrt_fusion), kind=kLoop, calls=%fused_computation.13 | loop fusion | flops 6291456 | bytes 6324736 | tf_op jit(solution)/shard_map/convert_element_type | solution.py:33
  27.7 5.0 %all-to-all-start = ((bf16[128,8,1024]{2,0,1:T(8,128)(2,1)}), bf16[128,8,1024]{2,0,1:T(8,128)(2,1)S(1)}, u32[]{:S(2)}, u32[]{:S(2)}) async-start(bf16[128,8,1024]{2,0,1:T(8,128)(2,1)} %multiply_convert_fusion.1), calls=%async_computation | async-start | bytes 4194304 | tf_op jit(solution)/shard_map/all_to_all | solution.py:36
  32.7 0.0 all-gather.5.cloned.1.call-start
  32.8 173.5 %all-gather.7.cloned.1.call-done = bf16[1,8192,512]{2,1,0:T(8,128)(2,1)} async-done(((bf16[1,2048,512]{2,1,0:T(8,128)(2,1)}), bf16[1,8192,512]{2,1,0:T(8,128)(2,1)}) %all-gather.7.cloned.1.call-update) | async-done | bytes 8388624 | tf_op jit(solution)/shard_map/all_gather | solution.py:20
  206.3 0.0 copy-done.3
  206.3 6.0 %multiply_convert_fusion.9 = (bf16[128,512]{1,0:T(8,128)(2,1)}, bf16[128,512]{1,0:T(8,128)(2,1)S(1)}) fusion(bf16[1,128,512]{2,1,0:T(8,128)(2,1)S(1)} %copy-done.3, bf16[1,8192,512]{2,1,0:T(8,128)(2,1)} %all-gather.7.cloned.1.call-done, bf16[1,128,8192]{2,1,0:T(8,128)(2,1)} %param.4, f32[8192]{0:T(1024)S(1)} %bitcast.59, f32[128]{0:T(128)S(1)} %add_rsqrt_fusion), kind=kOutput, calls=%fused_computation.21 | convolution fusion | flops 1078394880 | bytes 10912256 | tf_op jit(solution)/shard_map/dot_general | solution.py:27
  212.3 0.0 all-gather.5.cloned.1.call-update
  212.3 0.0 all-reduce.4.cloned.1.call-start
  212.4 0.0 all-to-all-done
  212.4 37.1 %all-gather.5.cloned.1.call-done = bf16[1024,512]{1,0:T(8,128)(2,1)} async-done(((bf16[128,512]{1,0:T(8,128)(2,1)}), bf16[1024,512]{1,0:T(8,128)(2,1)}) %all-gather.5.cloned.1.call-update) | async-done | bytes 1048592 | tf_op jit(solution)/shard_map/all_gather | solution.py:40
  249.5 4.9 %convert_multiply_fusion = (f32[1024,512]{1,0:T(8,128)}, f32[1024,512]{1,0:T(8,128)}) fusion(bf16[1,2048,512]{2,1,0:T(8,128)(2,1)} %param.6, s32[]{:T(128)S(6)} %select_n.7, bf16[1024,1024]{1,0:T(8,128)(2,1)S(1)} %bitcast.57, bf16[1024,512]{1,0:T(8,128)(2,1)} %all-gather.5.cloned.1.call-done), kind=kOutput, calls=%fused_computation.14 | convolution fusion | flops 1074790400 | bytes 8388612 | tf_op jit(solution)/shard_map/td,th->dh/dot_general | solution.py:37
  254.4 0.0 copy-start.2
  254.4 0.0 copy-start.1
  254.4 0.0 all-reduce.4.cloned.1.call-update
  254.4 0.7 copy-done.2
  255.1 0.9 copy-done.1
  256.0 6.2 %fusion.10 = bf16[8192]{0:T(1024)(128)(2,1)S(1)} fusion(f32[128]{0:T(128)S(1)} %add_rsqrt_fusion, bf16[1,128,8192]{2,1,0:T(8,128)(2,1)S(1)} %copy-done.1, bf16[128,512]{1,0:T(8,128)(2,1)S(1)} %get-tuple-element.7, bf16[1,8192,512]{2,1,0:T(8,128)(2,1)} %all-gather.7.cloned.1.call-done), kind=kOutput, calls=%fused_computation.17 | convolution fusion | flops 1080025088 | bytes 10633728 | tf_op jit(solution)/shard_map/th,dh->td/dot_general | solution.py:30
  262.2 26.9 %psum.37 = bf16[8192]{0:T(1024)(128)(2,1)S(1)} all-reduce(bf16[8192]{0:T(1024)(128)(2,1)S(1)} %fusion.10), channel_id=1, replica_groups=mesh['template'=4,'fsdp'=4,'dp'=2] {'fsdp','dp'}, use_global_device_ids=true, to_apply=%region_4.0 | all-reduce | flops 8192 | bytes 32768 | tf_op jit(solution)/shard_map/psum | solution.py:43
  289.1 14.8 %all-reduce = (f32[1024,1]{0,1:T(1,128)S(1)}, f32[1024,1]{0,1:T(1,128)S(1)}) all-reduce(f32[1024,1]{0,1:T(1,128)S(1)} %bitcast.61, f32[1024,1]{0,1:T(1,128)S(1)} %bitcast.62), channel_id=1, replica_groups=mesh['template'=4,'fsdp'=4,'dp'=2] {'template'}, use_global_device_ids=true, to_apply=%region_5.0 | all-reduce | flops 2048 | bytes 16384 | tf_op jit(solution)/shard_map/psum | solution.py:52
  303.9 0.6 div.18
  304.5 35.3 %all-reduce.4.cloned.1.call-done = (f32[1024,512]{1,0:T(8,128)}, f32[1024,512]{1,0:T(8,128)}) async-done(((f32[1024,512]{1,0:T(8,128)}, f32[1024,512]{1,0:T(8,128)}), (f32[1024,512]{1,0:T(8,128)}, f32[1024,512]{1,0:T(8,128)})) %all-reduce.4.cloned.1.call-update) | async-done | bytes 4194320 | tf_op jit(solution)/shard_map/psum | solution.py:52
  339.8 4.0 %div.17 = f32[1024,512]{1,0:T(8,128)} divide(f32[1024,512]{1,0:T(8,128)} %get-tuple-element.4, f32[1024,512]{1,0:T(8,128)} %get-tuple-element.5) | non-fusion elementwise | flops 524288 | bytes 6291456 | tf_op jit(solution)/shard_map/div | solution.py:53
  (6 shorter events, 0.1 us)
Async XLA Ops:
  7.2 16.3 %copy-start = (bf16[1,128,8192]{2,1,0:T(8,128)(2,1)S(1)}, bf16[1,128,8192]{2,1,0:T(8,128)(2,1)}, u32[]{:S(2)}) copy-start(bf16[1,128,8192]{2,1,0:T(8,128)(2,1)} %param.4) | copy-start | bytes 6291460
  7.2 199.1 %all-gather.7.cloned.1.call-start = ((), (), s32[]{:S(2)}) async-start(), calls=%async_computation.2 | async-start | bytes 10485760 | tf_op jit(solution)/shard_map/all_gather | solution.py:20
  23.9 182.3 %copy-start.3 = (bf16[1,128,512]{2,1,0:T(8,128)(2,1)S(1)}, bf16[1,128,512]{2,1,0:T(8,128)(2,1)}, u32[]{:S(2)}) copy-start(bf16[1,128,512]{2,1,0:T(8,128)(2,1)} %param.5) | copy-start | bytes 393220
  27.7 184.7 %all-to-all-start = ((bf16[128,8,1024]{2,0,1:T(8,128)(2,1)}), bf16[128,8,1024]{2,0,1:T(8,128)(2,1)S(1)}, u32[]{:S(2)}, u32[]{:S(2)}) async-start(bf16[128,8,1024]{2,0,1:T(8,128)(2,1)} %multiply_convert_fusion.1), calls=%async_computation | async-start | bytes 4194304 | tf_op jit(solution)/shard_map/all_to_all | solution.py:36
  32.7 216.8 %all-gather.5.cloned.1.call-start = ((), (), s32[]{:S(2)}) async-start(), calls=%async_computation.1 | async-start | bytes 1179648 | tf_op jit(solution)/shard_map/all_gather | solution.py:40
  212.3 127.5 %all-reduce.4.cloned.1.call-start = ((), (), s32[]{:S(2)}) async-start(), calls=%async_computation.3 | async-start | bytes 8388608 | tf_op jit(solution)/shard_map/psum | solution.py:52
  254.4 0.7 copy-start.2
  254.4 1.6 copy-start.1
Sparse Core Ops, SparseCore 0:
  9.6 196.6 all-gather.6
  212.4 37.0 all-gather.4
  254.5 85.2 all-reduce.3
where the time goes:
time: 352 us; the launch traced here: 350 us
  waiting for transfers between devices  247 us (70%)
  blocking collectives  53.5 us (15%)
  matrix products  17.1 us (5%)
  between operations  13.8 us (4%)
  other arithmetic  9.03 us (3%)
  local copies, waits for them, and re-layouts  5.2 us (1%)
  starting transfers between devices  5.12 us (1%)
    all_gather x1, waiting for transfers between devices, body(): lax.all_gather(w_shard, 'fsdp', axis=0, tiled=True)  173 us
    all_gather x1, waiting for transfers between devices, body(): lax.all_gather(sq_delta, ('fsdp', 'dp'), axis=0, tiled=True)  37.1 us
    psum x1, waiting for transfers between devices, body(): lax.psum((weighted, fisher, gain_weighted, gain_column), 'template')  35.3 us
    psum x1, blocking collectives, body(): lax.psum(gain_information.astype(jnp.bfloat16), ('fsdp', 'dp'))  26.9 us
    psum x1, blocking collectives, body(): lax.psum((weighted, fisher, gain_weighted, gain_column), 'template')  14.8 us
    all_gather x1, blocking collectives, body(): lax.all_gather(g_shard, 'fsdp', axis=0, tiled=True)  11.8 us
  transfers between devices with their start and end apart: 4, of which 3 were waited for; matrix products, arithmetic and copies ran while one was open for 6% of the time, Pallas kernels for 0%

commit v1 on v0

v1 whole, which is shorter than its diff:
```python
import functools
import math

import jax
import jax.numpy as jnp
from jax import lax
from jax.experimental import pallas as pl
from jax.experimental.pallas import tpu as pltpu
from jax.sharding import PartitionSpec as P

F32 = jnp.float32
BF16 = jnp.bfloat16
MESH = pl.DeviceIdType.MESH


def flip(a, k):
    b = 1
    while b <= k:
        if k & b:
            a = a + b - 2 * b * ((a // b) % 2)
        b *= 2
    return a


def far_first(n):
    return list(range(n // 2, n)) + list(range(1, n // 2))


def kernel(T, Z, X, h_ref, t_ref, w_ref, g_ref, o_ref, og_ref,
           recv, xbuf, rmine, rz, rx, rcol, ps, rs, dall, sqt, fsend, frecv,
           f1send, f1recv, wq, gbuf,
           h_ss, h_rs, r_ss, r_rs, x_ss, x_rs, rx_ss, rx_rs, p_ss, p_rs,
           d_ss, d_rs, e_ss, e_rs, w_ss, w_rs, f_ss, f_rs, g_ss, g_rs, o_ss, o_rs):
    m, z, x = (lax.axis_index(a) for a in ("template", "fsdp", "dp"))
    tb, D = h_ref.shape
    FS, H = w_ref.shape
    mine = FS // X
    Q = mine // T
    scale = 1.0 / math.sqrt(D)
    pending = []

    def zdev(k):
        return (m, flip(z, k), x)

    def xdev(k):
        return (m, z, flip(x, k))

    def tdev(k):
        return (flip(m, k), z, x)

    def send(src, dst, ss, rs_, dev):
        c = pltpu.make_async_remote_copy(src_ref=src, dst_ref=dst, send_sem=ss, recv_sem=rs_,
                                         device_id=dev, device_id_type=MESH)
        c.start()
        pending.append(c)

    def arrived(dst, sem):
        pltpu.make_async_copy(dst, dst, sem).wait()

    def rows(s):
        return pl.ds(s * tb, tb)

    def cols(a, width):
        return pl.ds(pl.multiple_of(a * width, width), width)

    peers = ([zdev(k) for k in range(1, Z)] + [xdev(k) for k in range(1, X)]
             + [tdev(k) for k in range(1, T)])
    barrier = pltpu.get_barrier_semaphore()
    for dev in peers:
        pl.semaphore_signal(barrier, inc=1, device_id=dev, device_id_type=MESH)
    pl.semaphore_wait(barrier, len(peers))

    for k in far_first(Z):
        send(h_ref.at[:, cols(flip(z, k), FS)], recv.at[k], h_ss.at[k], h_rs.at[k], zdev(k))
    for j in range(1, X):
        send(h_ref.at[:, cols(z * X + flip(x, j), mine)], xbuf.at[rows(j * Z)],
             x_ss.at[j * Z], x_rs.at[j * Z], xdev(j))
    for k in range(1, T):
        send(w_ref.at[cols(x * T + flip(m, k), Q)], wq.at[k], w_ss.at[k], w_rs.at[k], tdev(k))

    step = min(512, D)

    def add_squares(i, acc):
        c = h_ref[:, cols(i, step)].astype(F32)
        c = c * c
        for a in range(0, step, 128):
            acc = acc + c[:, a:a + 128]
        return acc

    acc = lax.fori_loop(0, D // step, add_squares, jnp.zeros((tb, 128), F32))
    ratio = lax.rsqrt(jnp.sum(acc, axis=1, keepdims=True) / D + 1e-05)
    full = jnp.broadcast_to(ratio, (tb, 128))
    rcol[rows(0), :] = full
    rmine[...] = full.T[0:8, :]
    for k in far_first(Z):
        send(rmine, rz.at[k], r_ss.at[k], r_rs.at[k], zdev(k))
    for j in range(1, X):
        send(rmine, rx.at[j * Z], rx_ss.at[j * Z], rx_rs.at[j * Z], xdev(j))

    def column(row_ref):
        return jnp.broadcast_to(row_ref[0:1, :], (128, 128)).T

    wstep = min(512, FS)

    def partial(block, first, slot):
        r = rcol[rows(slot), 0:1]

        def body(i, total):
            here = cols(i, wstep)
            there = pl.ds(pl.multiple_of(first + i * wstep, wstep), wstep)
            c = (block[:, there].astype(F32) * r * g_ref[:, here].astype(F32)).astype(BF16)
            return total + jnp.dot(c, w_ref[here, :], preferred_element_type=F32)

        return lax.fori_loop(0, FS // wstep, body, jnp.zeros((tb, H), F32))

    own = partial(h_ref, z * FS, 0)
    order = list(range(1, Z))
    for k in order:
        arrived(rz.at[k], r_rs.at[k])
        arrived(recv.at[k], h_rs.at[k])
        for j in range(1, X):
            send(recv.at[k, :, cols(flip(x, j), mine)], xbuf.at[rows(j * Z + k)],
                 x_ss.at[j * Z + k], x_rs.at[j * Z + k], xdev(j))
            send(rz.at[k], rx.at[j * Z + k], rx_ss.at[j * Z + k], rx_rs.at[j * Z + k], xdev(j))
        rcol[rows(k), :] = column(rz.at[k])
        ps[k] = partial(recv.at[k], 0, k).astype(BF16)
        send(ps.at[k], rs.at[k], p_ss.at[k], p_rs.at[k], zdev(k))

    gain = g_ref[:, cols(x, mine)].astype(F32)
    fstep = min(256, mine)

    def square_slot(slot):
        r = rcol[rows(slot), 0:1]

        def body(i, _):
            here = cols(i, fstep)
            g = g_ref[:, pl.ds(pl.multiple_of(x * mine + i * fstep, fstep), fstep)].astype(F32)
            n = (xbuf[rows(slot), here].astype(F32) * r * g).astype(BF16).astype(F32)
            sqt[here, slot * tb:(slot + 1) * tb] = (n * n).T.astype(BF16)
            return 0

        lax.fori_loop(0, mine // fstep, body, 0)

    xbuf[rows(0), :] = h_ref[:, cols(z * X + x, mine)]
    square_slot(0)
    for k in order:
        xbuf[rows(k), :] = recv[k, :, cols(x, mine)]
        square_slot(k)

    values = own
    for k in order:
        arrived(rs.at[k], p_rs.at[k])
        values = values + rs[k].astype(F32)
    dall[rows(0), :] = (values * scale - t_ref[...].astype(F32)).astype(BF16)
    for k in far_first(Z):
        send(dall.at[rows(0)], dall.at[rows(k)], d_ss.at[k], d_rs.at[k], zdev(k))
    for j in range(1, X):
        send(dall.at[rows(0)], dall.at[rows(j * Z)], e_ss.at[j * Z], e_rs.at[j * Z], xdev(j))
    for j in range(1, X):
        for k in range(Z):
            s = j * Z + k
            arrived(rx.at[s], rx_rs.at[s])
            arrived(xbuf.at[rows(s)], x_rs.at[s])
            rcol[rows(s), :] = column(rx.at[s])
            square_slot(s)
    for k in order:
        arrived(dall.at[rows(k)], d_rs.at[k])
        for j in range(1, X):
            s = j * Z + k
            send(dall.at[rows(k)], dall.at[rows(s)], e_ss.at[s], e_rs.at[s], xdev(j))
    for j in range(1, X):
        for k in range(Z):
            s = j * Z + k
            arrived(dall.at[rows(s)], e_rs.at[s])

    tokens = X * Z * tb
    tstep = min(512, tokens)

    def fisher(q):
        def body(i, total):
            here = cols(i, tstep)
            d = dall[here, :].astype(F32)
            return total + jnp.dot(sqt[cols(q, Q), here], (d * d).astype(BF16),
                                   preferred_element_type=F32)

        return lax.fori_loop(0, tokens // tstep, body, jnp.zeros((Q, H), F32))

    for k in far_first(T):
        if k == 1:
            f1send[...] = fisher(flip(m, k))
            send(f1send, f1recv, f_ss.at[k], f_rs.at[k], tdev(k))
        else:
            fsend[k] = fisher(flip(m, k)).astype(BF16)
            send(fsend.at[k], frecv.at[k], f_ss.at[k], f_rs.at[k], tdev(k))
    den = fisher(m)
    num = den * w_ref[cols(x * T + m, Q), :].astype(F32)

    def back_slot(s, total):
        here = cols(s, tb)
        b = lax.dot_general(dall[here, :], w_ref[cols(x, mine), :], (((1,), (1,)), ((), ())),
                            preferred_element_type=F32) * scale
        b = b * (xbuf[here, :].astype(F32) * rcol[here, 0:1])
        return total + jnp.sum(b * b, axis=0, keepdims=True)

    gfish = lax.fori_loop(0, X * Z, back_slot, jnp.zeros((1, mine), F32))
    gbuf[0, 0:1, :] = gfish * gain
    gbuf[0, 1:2, :] = gfish
    gbuf[0, 2:8, :] = jnp.zeros((6, mine), F32)
    for k in range(1, T):
        send(gbuf.at[0], gbuf.at[k], g_ss.at[k], g_rs.at[k], tdev(k))

    for k in range(1, T):
        arrived(wq.at[k], w_rs.at[k])
        if k == 1:
            arrived(f1recv, f_rs.at[k])
            f = f1recv[...]
        else:
            arrived(frecv.at[k], f_rs.at[k])
            f = frecv[k].astype(F32)
        den = den + f
        num = num + f * wq[k].astype(F32)
    o_ref[cols(m, Q), :] = num / den
    held = [0]
    b = T // 2
    while b:
        for j in held:
            block = o_ref.at[cols(flip(m, j), Q)]
            send(block, block, o_ss.at[j ^ b], o_rs.at[j ^ b], tdev(b))
        for j in held:
            arrived(o_ref.at[cols(flip(m, j ^ b), Q)], o_rs.at[j ^ b])
        held = held + [j ^ b for j in held]
        b //= 2

    for k in range(1, T):
        arrived(gbuf.at[k], g_rs.at[k])
    sums = [gbuf[k] for k in range(T)]
    while len(sums) > 1:
        sums = [sums[i] + sums[i + 1] for i in range(0, len(sums), 2)]
    og_ref[...] = sums[0][0:1, :] / sums[0][1:2, :]
    for c in pending:
        c.wait_send()


def body(T, Z, X, hidden, target, weight, gain):
    _, tb, D = hidden.shape
    _, FS, H = weight.shape
    mine = FS // X
    Q = mine // T
    S = X * Z
    dma = lambda n: pltpu.SemaphoreType.DMA((n,))
    vmem = pltpu.VMEM
    flops = 2 * S * tb * mine * H * 3
    merged, merged_gain = pl.pallas_call(
        functools.partial(kernel, T, Z, X),
        out_shape=(jax.ShapeDtypeStruct((mine, H), F32), jax.ShapeDtypeStruct((1, mine), F32)),
        in_specs=[pl.BlockSpec(memory_space=pltpu.VMEM)] * 4,
        out_specs=[pl.BlockSpec(memory_space=pltpu.VMEM)] * 2,
        scratch_shapes=[
            vmem((Z, tb, FS), BF16),
            vmem((S * tb, mine), BF16),
            vmem((8, 128), F32),
            vmem((Z, 8, 128), F32),
            vmem((S, 8, 128), F32),
            vmem((S * tb, 128), F32),
            vmem((Z, tb, H), BF16),
            vmem((Z, tb, H), BF16),
            vmem((S * tb, H), BF16),
            vmem((mine, S * tb), BF16),
            vmem((T, Q, H), BF16),
            vmem((T, Q, H), BF16),
            vmem((Q, H), F32),
            vmem((Q, H), F32),
            vmem((T, Q, H), BF16),
            vmem((T, 8, mine), F32),
            dma(Z), dma(Z), dma(Z), dma(Z), dma(S), dma(S), dma(S), dma(S), dma(Z), dma(Z),
            dma(Z), dma(Z), dma(S), dma(S), dma(T), dma(T), dma(T), dma(T), dma(T), dma(T),
            dma(T), dma(T),
        ],
        cost_estimate=pl.CostEstimate(flops=flops, bytes_accessed=8 << 20, transcendentals=0),
        compiler_params=pltpu.CompilerParams(
            collective_id=0, has_side_effects=True, vmem_limit_bytes=56 << 20),
    )(hidden[0], target[0], weight[0], gain)
    return merged, merged_gain[0]


def solution(mesh):
    T, Z, X = (mesh.shape[a] for a in ("template", "fsdp", "dp"))
    in_specs = (
        P("template", ("fsdp", "dp"), None),
        P("template", ("fsdp", "dp"), None),
        P("template", "fsdp", None),
        P("template", "fsdp"),
    )
    out_specs = (P(("fsdp", "dp"), None), P(("fsdp", "dp")))
    return jax.shard_map(functools.partial(body, T, Z, X), mesh=mesh, in_specs=in_specs,
                         out_specs=out_specs, check_vma=False)
```

time: 352 us -> 120 us (0.34)
  the two profiles are of different devices: /device:TPU:1 before, /device:TPU:25 now
where the time goes in v1:
time: 120 us
  Pallas kernels  116 us (97%)
  local copies, waits for them, and re-layouts  3.68 us (3%)
    pallas_call x1, Pallas kernels, body(): pl.pallas_call(functools.partial(kernel, T, Z, X), out_shape=(jax.ShapeDt...  116 us
    unnamed x4, local copies, waits for them, and re-layouts  3.68 us

profile of v1, /device:TPU:25, one launch (start us, length us, event | category | flops | bytes accessed | tf_op | source)
XLA Modules:
  0.0 120.0 jit_solution(466680272149323881)
XLA Ops:
  0.6 115.7 %shard_map.59 = (f32[1024,512]{1,0:T(8,128)}, f32[1,1024]{1,0:T(1,128)}) custom-call(bf16[128,8192]{1,0:T(8,128)(2,1)} %bitcast.5, bf16[128,512]{1,0:T(8,128)(2,1)} %bitcast.7, bf16[2048,512]{1,0:T(8,128)(2,1)} %bitcast.6, bf16[1,2048]{1,0:T(2,128)(2,1)} %g_ref.1), custom_call_target="tpu_custom_call" | custom-call | flops 3221225472 | bytes 8388608 | tf_op jit(solution)/shard_map/pallas_call | solution.py:253
  116.3 0.0 copy-start
  116.3 3.1 %copy.8 = f32[1024,512]{1,0:T(8,128)} copy(f32[1024,512]{1,0:T(8,128)} %get-tuple-element.8) | data formatting | bytes 4194304
  119.4 0.0 copy-done
  119.4 0.6 copy.9
Async XLA Ops:
  116.3 3.1 %copy-start = (f32[1,1024]{1,0:T(1,128)S(1)}, f32[1,1024]{1,0:T(1,128)}, u32[]{:S(2)}) copy-start(f32[1,1024]{1,0:T(1,128)} %get-tuple-element.5) | copy-start | bytes 12292

commit v2 on v1

v2 whole, which is shorter than its diff:
```python
import functools
import math

import jax
import jax.numpy as jnp
from jax import lax
from jax.experimental import pallas as pl
from jax.experimental.pallas import tpu as pltpu
from jax.sharding import PartitionSpec as P

F32 = jnp.float32
BF16 = jnp.bfloat16
MESH = pl.DeviceIdType.MESH


def flip(a, k):
    b = 1
    while b <= k:
        if k & b:
            a = a + b - 2 * b * ((a // b) % 2)
        b *= 2
    return a


def far_first(n):
    return list(range(n // 2, n)) + list(range(1, n // 2))


def backward_bits(p, n):
    k, b = 0, n // 2
    while b:
        if p & 1:
            k += b
        p //= 2
        b //= 2
    return k


def kernel(T, Z, X, C, U, h_ref, t_ref, w_ref, g_ref, o_ref, og_ref,
           recv, xbuf, rz, rx, rcol, pacc, ps, rs, dall, sqt, facc, fsend, frecv,
           f1send, f1recv, wq, gbuf,
           h_ss, h_rs, r_ss, r_rs, x_ss, x_rs, rx_ss, rx_rs, p_ss, p_rs,
           d_ss, d_rs, e_ss, e_rs, w_ss, w_rs, f_ss, f_rs, g_ss, g_rs, o_ss, o_rs):
    m, z, x = (lax.axis_index(a) for a in ("template", "fsdp", "dp"))
    tb, D = h_ref.shape
    FS, H = w_ref.shape
    mine = FS // X
    Q = mine // T
    QU = Q // U
    tc = tb // C
    ZR = Z * tc
    NR = X * ZR
    scale = 1.0 / math.sqrt(D)
    pending = []

    def zdev(k):
        return (m, flip(z, k), x)

    def xdev(k):
        return (m, z, flip(x, k))

    def tdev(k):
        return (flip(m, k), z, x)

    def send(src, dst, ss, rs_, dev):
        c = pltpu.make_async_remote_copy(src_ref=src, dst_ref=dst, send_sem=ss, recv_sem=rs_,
                                         device_id=dev, device_id_type=MESH)
        c.start()
        pending.append(c)

    def arrived(dst, sem):
        pltpu.make_async_copy(dst, dst, sem).wait()

    def cols(a, width):
        return pl.ds(pl.multiple_of(a * width, width), width)

    def at(first, n):
        return pl.ds(first, n)

    peers = ([zdev(k) for k in range(1, Z)] + [xdev(k) for k in range(1, X)]
             + [tdev(k) for k in range(1, T)])
    barrier = pltpu.get_barrier_semaphore()
    for dev in peers:
        pl.semaphore_signal(barrier, inc=1, device_id=dev, device_id_type=MESH)
    pl.semaphore_wait(barrier, len(peers))

    def send_hidden(c):
        for p in sorted(range(1, Z), key=lambda p: -(p & 1)):
            k = backward_bits(p, Z)
            send(h_ref.at[at(c * tc, tc), cols(flip(z, k), FS)], recv.at[at(c * ZR + p * tc, tc)],
                 h_ss.at[c * Z + p], h_rs.at[c * Z + p], zdev(k))

    send_hidden(0)

    step = min(512, D)

    def add_squares(i, acc):
        c = h_ref[:, cols(i, step)].astype(F32)
        c = c * c
        for a in range(0, step, 128):
            acc = acc + c[:, a:a + 128]
        return acc

    acc = lax.fori_loop(0, D // step, add_squares, jnp.zeros((tb, 128), F32))
    ratio = lax.rsqrt(jnp.sum(acc, axis=1, keepdims=True) / D + 1e-05)
    rz[0] = jnp.broadcast_to(ratio, (tb, 128)).T[0:8, :]
    for p in range(1, Z):
        k = backward_bits(p, Z)
        send(rz.at[0], rz.at[p], r_ss.at[p], r_rs.at[p], zdev(k))
    if C > 1:
        send_hidden(1)
    for k in range(1, T):
        send(w_ref.at[cols(x * T + flip(m, k), Q)], wq.at[k], w_ss.at[k], w_rs.at[k], tdev(k))

    def put_column(row_ref, j, p):
        col = jnp.broadcast_to(row_ref[0:1, :], (128, 128)).T
        for c in range(C):
            rcol[at((c * X + j) * ZR + p * tc, tc), :] = col[c * tc:(c + 1) * tc, :]

    wstep = min(512, FS)

    def partial(c):
        r = rcol[at(c * NR, ZR), 0:1]

        def body(i, total):
            here = cols(i, wstep)
            n = (recv[at(c * ZR, ZR), here].astype(F32) * r
                 * g_ref[:, here].astype(F32)).astype(BF16)
            return total + jnp.dot(n, w_ref[here, :], preferred_element_type=F32)

        pacc[...] = lax.fori_loop(0, FS // wstep, body, jnp.zeros((ZR, H), F32))

    fstep = min(256, mine)

    def squares(c, j):
        first = (c * X + j) * ZR
        r = rcol[at(first, ZR), 0:1]

        def body(i, _):
            here = cols(i, fstep)
            g = g_ref[:, pl.ds(pl.multiple_of(x * mine + i * fstep, fstep), fstep)].astype(F32)
            n = (xbuf[at(first, ZR), here].astype(F32) * r * g).astype(BF16).astype(F32)
            sqt[here, first:first + ZR] = (n * n).T.astype(BF16)
            return 0

        lax.fori_loop(0, mine // fstep, body, 0)

    def other_squares(c):
        for j in range(1, X):
            if c == 0:
                arrived(rx.at[j], rx_rs.at[j])
                for p in range(Z):
                    put_column(rx.at[j, p], j, p)
            arrived(xbuf.at[at((c * X + j) * ZR, ZR)], x_rs.at[c * X + j])
            squares(c, j)

    def residuals_here(c):
        for j in range(1, X):
            n = 0
            while n < Z:
                size = max(n, 1) * tc
                first = (c * X + j) * ZR + n * tc
                arrived(dall.at[at(first, size)], e_rs.at[(c * X + j) * Z + n])
                n = max(2 * n, 1)

    def forward(c, n):
        size = max(n, 1) * tc
        for j in range(1, X):
            send(dall.at[at(c * NR + n * tc, size)], dall.at[at((c * X + j) * ZR + n * tc, size)],
                 e_ss.at[(c * X + j) * Z + n], e_rs.at[(c * X + j) * Z + n], xdev(j))

    def fisher(c, first, size):
        d = dall[at(c * NR, NR), :].astype(F32)
        f = jnp.dot(sqt[pl.ds(first, size), c * NR:(c + 1) * NR], (d * d).astype(BF16),
                    preferred_element_type=F32)
        if c:
            f = f + facc[pl.ds(first, size), :]
        return f

    def add_fisher(c):
        size = min(256, mine)

        def body(i, _):
            first = pl.multiple_of(i * size, size)
            facc[pl.ds(first, size), :] = fisher(c, first, size)
            return 0

        lax.fori_loop(0, mine // size, body, 0)

    def back(c, total):
        def body(i, total):
            here = pl.ds(pl.multiple_of(c * NR + i * ZR, ZR), ZR)
            b = lax.dot_general(dall[here, :], w_ref[cols(x, mine), :], (((1,), (1,)), ((), ())),
                                preferred_element_type=F32) * scale
            b = b * (xbuf[here, :].astype(F32) * rcol[here, 0:1])
            return total + jnp.sum(b * b, axis=0, keepdims=True)

        return lax.fori_loop(0, X, body, total)

    gfish = jnp.zeros((1, mine), F32)
    for c in range(C):
        recv[at(c * ZR, tc), :] = h_ref[at(c * tc, tc), cols(z, FS)]
        if c == 0:
            put_column(rz.at[0], 0, 0)
            for p in range(1, Z):
                arrived(rz.at[p], r_rs.at[p])
                put_column(rz.at[p], 0, p)
            for j in range(1, X):
                send(rz, rx.at[j], rx_ss.at[j], rx_rs.at[j], xdev(j))
        for p in range(1, Z):
            arrived(recv.at[at(c * ZR + p * tc, tc)], h_rs.at[c * Z + p])
        if c + 2 < C:
            send_hidden(c + 2)
        for j in range(1, X):
            send(recv.at[at(c * ZR, ZR), cols(flip(x, j), mine)],
                 xbuf.at[at((c * X + j) * ZR, ZR)], x_ss.at[c * X + j], x_rs.at[c * X + j], xdev(j))
        partial(c)
        n, b = Z, 1
        while n > 1:
            half = n // 2
            size = half * tc
            there = at((c * Z + half) * tc, size)
            ps[there, :] = pacc[at(size, size), :].astype(BF16)
            send(ps.at[there], rs.at[there], p_ss.at[c * Z + half], p_rs.at[c * Z + half], zdev(b))
            if b == 1:
                xbuf[at(c * NR, ZR), :] = recv[at(c * ZR, ZR), cols(x, mine)]
                squares(c, 0)
            arrived(rs.at[there], p_rs.at[c * Z + half])
            pacc[at(0, size), :] += rs[there, :].astype(F32)
            n, b = half, b * 2
        dall[at(c * NR, tc), :] = (pacc[at(0, tc), :] * scale
                                   - t_ref[at(c * tc, tc), :].astype(F32)).astype(BF16)
        n, b = 1, Z // 2
        while n < Z:
            size = n * tc
            send(dall.at[at(c * NR, size)], dall.at[at(c * NR + size, size)],
                 d_ss.at[c * Z + n], d_rs.at[c * Z + n], zdev(b))
            if n == 1:
                forward(c, 0)
                if c:
                    residuals_here(c - 1)
                    add_fisher(c - 1)
                other_squares(c)
            arrived(dall.at[at(c * NR + size, size)], d_rs.at[c * Z + n])
            forward(c, n)
            n, b = 2 * n, b // 2
        if 0 < c < C - 1:
            gfish = back(c - 1, gfish)
    residuals_here(C - 1)

    for u in range(U):
        for k in far_first(T):
            f = fisher(C - 1, pl.multiple_of(flip(m, k) * Q + u * QU, QU), QU)
            i = k * U + u
            part = at(u * QU, QU)
            if k == 1:
                f1send[part, :] = f
                send(f1send.at[part], f1recv.at[part], f_ss.at[i], f_rs.at[i], tdev(k))
            else:
                fsend[k, part, :] = f.astype(BF16)
                send(fsend.at[k, part], frecv.at[k, part], f_ss.at[i], f_rs.at[i], tdev(k))
    for c in range(max(C - 2, 0), C):
        gfish = back(c, gfish)
    gbuf[0, 0:1, :] = gfish * g_ref[:, cols(x, mine)].astype(F32)
    gbuf[0, 1:2, :] = gfish
    gbuf[0, 2:8, :] = jnp.zeros((6, mine), F32)
    for k in range(1, T):
        send(gbuf.at[0], gbuf.at[k], g_ss.at[k], g_rs.at[k], tdev(k))

    def block(j, u):
        return o_ref.at[pl.ds(pl.multiple_of(flip(m, j) * Q + u * QU, QU), QU)]

    def share(j, b, u):
        i = (j ^ b) * U + u
        send(block(j, u), block(j, u), o_ss.at[i], o_rs.at[i], tdev(b))

    for u in range(U):
        first = pl.multiple_of(m * Q + u * QU, QU)
        part = at(u * QU, QU)
        den = fisher(C - 1, first, QU)
        num = den * w_ref[pl.ds(pl.multiple_of(x * mine + m * Q + u * QU, QU), QU), :].astype(F32)
        for k in range(1, T):
            if u == 0:
                arrived(wq.at[k], w_rs.at[k])
            i = k * U + u
            if k == 1:
                arrived(f1recv.at[part], f_rs.at[i])
                f = f1recv[part, :]
            else:
                arrived(frecv.at[k, part], f_rs.at[i])
                f = frecv[k, part, :].astype(F32)
            den = den + f
            num = num + f * wq[k, part, :].astype(F32)
        o_ref[pl.ds(first, QU), :] = num / den
        share(0, T // 2, u)
    held, b = [0], T // 2
    while b > 1:
        for u in range(U):
            for j in held:
                arrived(block(j ^ b, u), o_rs.at[(j ^ b) * U + u])
                share(j, b // 2, u)
                share(j ^ b, b // 2, u)
        held = held + [j ^ b for j in held]
        b //= 2

    for k in range(1, T):
        arrived(gbuf.at[k], g_rs.at[k])
    sums = [gbuf[k] for k in range(T)]
    while len(sums) > 1:
        sums = [sums[i] + sums[i + 1] for i in range(0, len(sums), 2)]
    og_ref[...] = sums[0][0:1, :] / sums[0][1:2, :]
    for u in range(U):
        for j in held:
            arrived(block(j ^ 1, u), o_rs.at[(j ^ 1) * U + u])
    for c in pending:
        c.wait_send()


def body(T, Z, X, hidden, target, weight, gain):
    _, tb, D = hidden.shape
    _, FS, H = weight.shape
    mine = FS // X
    Q = mine // T
    S = X * Z
    C = 4
    U = 2 if Q >= 64 else 1
    dma = lambda n: pltpu.SemaphoreType.DMA((n,))
    vmem = pltpu.VMEM
    flops = 2 * S * tb * mine * H * 3
    merged, merged_gain = pl.pallas_call(
        functools.partial(kernel, T, Z, X, C, U),
        out_shape=(jax.ShapeDtypeStruct((mine, H), F32), jax.ShapeDtypeStruct((1, mine), F32)),
        in_specs=[pl.BlockSpec(memory_space=pltpu.VMEM)] * 4,
        out_specs=[pl.BlockSpec(memory_space=pltpu.VMEM)] * 2,
        scratch_shapes=[
            vmem((Z * tb, FS), BF16),
            vmem((S * tb, mine), BF16),
            vmem((Z, 8, 128), F32),
            vmem((X, Z, 8, 128), F32),
            vmem((S * tb, 128), F32),
            vmem((Z * tb // C, H), F32),
            vmem((Z * tb, H), BF16),
            vmem((Z * tb, H), BF16),
            vmem((S * tb, H), BF16),
            vmem((mine, S * tb), BF16),
            vmem((mine, H), F32),
            vmem((T, Q, H), BF16),
            vmem((T, Q, H), BF16),
            vmem((Q, H), F32),
            vmem((Q, H), F32),
            vmem((T, Q, H), BF16),
            vmem((T, 8, mine), F32),
            dma(C * Z), dma(C * Z), dma(Z), dma(Z), dma(C * X), dma(C * X), dma(X), dma(X),
            dma(C * Z), dma(C * Z), dma(C * Z), dma(C * Z), dma(C * S), dma(C * S),
            dma(T), dma(T), dma(T * U), dma(T * U), dma(T), dma(T), dma(T * U), dma(T * U),
        ],
        cost_estimate=pl.CostEstimate(flops=flops, bytes_accessed=8 << 20, transcendentals=0),
        compiler_params=pltpu.CompilerParams(
            collective_id=0, has_side_effects=True, vmem_limit_bytes=56 << 20),
    )(hidden[0], target[0], weight[0], gain)
    return merged, merged_gain[0]


def solution(mesh):
    T, Z, X = (mesh.shape[a] for a in ("template", "fsdp", "dp"))
    in_specs = (
        P("template", ("fsdp", "dp"), None),
        P("template", ("fsdp", "dp"), None),
        P("template", "fsdp", None),
        P("template", "fsdp"),
    )
    out_specs = (P(("fsdp", "dp"), None), P(("fsdp", "dp")))
    return jax.shard_map(functools.partial(body, T, Z, X), mesh=mesh, in_specs=in_specs,
                         out_specs=out_specs, check_vma=False)
```

time: 120 us -> 135 us (1.12)
  the two profiles are of different devices: /device:TPU:25 before, /device:TPU:1 now
where the time goes in v2:
time: 135 us
  Pallas kernels  131 us (97%)
  local copies, waits for them, and re-layouts  3.68 us (3%)
    pallas_call x1, Pallas kernels, body(): pl.pallas_call(functools.partial(kernel, T, Z, X, C, U), out_shape=(jax.S...  131 us
    unnamed x4, local copies, waits for them, and re-layouts  3.68 us

profile of v2, /device:TPU:1, one launch (start us, length us, event | category | flops | bytes accessed | tf_op | source)
XLA Modules:
  0.0 135.1 jit_solution(9190944814805416711)
XLA Ops:
  0.6 130.7 %shard_map.59 = (f32[1024,512]{1,0:T(8,128)}, f32[1,1024]{1,0:T(1,128)}) custom-call(bf16[128,8192]{1,0:T(8,128)(2,1)} %bitcast.5, bf16[128,512]{1,0:T(8,128)(2,1)} %bitcast.7, bf16[2048,512]{1,0:T(8,128)(2,1)} %bitcast.6, bf16[1,2048]{1,0:T(2,128)(2,1)} %g_ref.1), custom_call_target="tpu_custom_call" | custom-call | flops 3221225472 | bytes 8388608 | tf_op jit(solution)/shard_map/pallas_call | solution.py:330
  131.4 0.0 copy-start
  131.4 3.1 %copy.8 = f32[1024,512]{1,0:T(8,128)} copy(f32[1024,512]{1,0:T(8,128)} %get-tuple-element.8) | data formatting | bytes 4194304
  134.5 0.0 copy-done
  134.5 0.6 copy.9
Async XLA Ops:
  131.4 3.1 %copy-start = (f32[1,1024]{1,0:T(1,128)S(1)}, f32[1,1024]{1,0:T(1,128)}, u32[]{:S(2)}) copy-start(f32[1,1024]{1,0:T(1,128)} %get-tuple-element.5) | copy-start | bytes 12292

commit v3 on v1

v3 whole, which is shorter than its diff:
```python
import functools
import math

import jax
import jax.numpy as jnp
from jax import lax
from jax.experimental import pallas as pl
from jax.experimental.pallas import tpu as pltpu
from jax.sharding import PartitionSpec as P

F32 = jnp.float32
BF16 = jnp.bfloat16
MESH = pl.DeviceIdType.MESH


def flip(a, k):
    b = 1
    while b <= k:
        if k & b:
            a = a + b - 2 * b * ((a // b) % 2)
        b *= 2
    return a


def far_first(n):
    return list(range(n // 2, n)) + list(range(1, n // 2))


def kernel(T, Z, X, C, B, h_ref, t_ref, w_ref, g_ref, o_ref, og_ref,
           recv, xbuf, rz, rx, rcol, own, ps, rs, dall, sqt, fsend, frecv,
           f1send, f1recv, wq, gbuf,
           h_ss, h_rs, r_ss, r_rs, x_ss, x_rs, rx_ss, rx_rs, p_ss, p_rs,
           d_ss, d_rs, e_ss, e_rs, w_ss, w_rs, f_ss, f_rs, g_ss, g_rs, o_ss, o_rs):
    m, z, x = (lax.axis_index(a) for a in ("template", "fsdp", "dp"))
    tb, D = h_ref.shape
    FS, H = w_ref.shape
    mine = FS // X
    Q = mine // T
    tc = tb // C
    ZR = Z * tc
    HB = H // B
    tokens = C * X * ZR
    scale = 1.0 / math.sqrt(D)
    pending = []

    def zdev(k):
        return (m, flip(z, k), x)

    def xdev(k):
        return (m, z, flip(x, k))

    def tdev(k):
        return (flip(m, k), z, x)

    def send(src, dst, ss, rs_, dev):
        c = pltpu.make_async_remote_copy(src_ref=src, dst_ref=dst, send_sem=ss, recv_sem=rs_,
                                         device_id=dev, device_id_type=MESH)
        c.start()
        pending.append(c)

    def arrived(dst, sem):
        pltpu.make_async_copy(dst, dst, sem).wait()

    def cols(a, width):
        return pl.ds(pl.multiple_of(a * width, width), width)

    peers = ([zdev(k) for k in range(1, Z)] + [xdev(k) for k in range(1, X)]
             + [tdev(k) for k in range(1, T)])
    barrier = pltpu.get_barrier_semaphore()
    for dev in peers:
        pl.semaphore_signal(barrier, inc=1, device_id=dev, device_id_type=MESH)
    pl.semaphore_wait(barrier, len(peers))

    for c in range(C):
        for k in far_first(Z):
            send(h_ref.at[pl.ds(c * tc, tc), cols(flip(z, k), FS)], recv.at[c, k],
                 h_ss.at[c * Z + k], h_rs.at[c * Z + k], zdev(k))

    step = min(512, D)

    def add_squares(i, acc):
        c = h_ref[:, cols(i, step)].astype(F32)
        c = c * c
        for a in range(0, step, 128):
            acc = acc + c[:, a:a + 128]
        return acc

    acc = lax.fori_loop(0, D // step, add_squares, jnp.zeros((tb, 128), F32))
    ratio = lax.rsqrt(jnp.sum(acc, axis=1, keepdims=True) / D + 1e-05)
    rz[0] = jnp.broadcast_to(ratio, (tb, 128)).T[0:8, :]
    for k in far_first(Z):
        send(rz.at[0], rz.at[k], r_ss.at[k], r_rs.at[k], zdev(k))
    for k in range(1, T):
        send(w_ref.at[cols(x * T + flip(m, k), Q)], wq.at[k], w_ss.at[k], w_rs.at[k], tdev(k))

    def put_column(row_ref, j, k):
        col = jnp.broadcast_to(row_ref[0:1, :], (128, 128)).T
        for c in range(C):
            rcol[c, j, k] = col[c * tc:(c + 1) * tc, :]

    wstep = min(512, FS)

    def partial(c):
        r = rcol[c, 0].reshape(ZR, 128)[:, 0:1]

        def body(i, total):
            here = cols(i, wstep)
            n = (recv[c, :, :, here].reshape(ZR, wstep).astype(F32) * r
                 * g_ref[:, here].astype(F32)).astype(BF16)
            return total + jnp.dot(n, w_ref[here, :], preferred_element_type=F32)

        v = lax.fori_loop(0, FS // wstep, body, jnp.zeros((ZR, H), F32))
        own[pl.ds(c * tc, tc), :] = v[0:tc, :]
        for i in range(B):
            for k in range(1, Z):
                ps[i, k, pl.ds(c * tc, tc), :] = (
                    v[k * tc:(k + 1) * tc, i * HB:(i + 1) * HB].astype(BF16))

    fstep = min(256, mine)

    def squares(c, j):
        r = rcol[c, j].reshape(ZR, 128)[:, 0:1]
        first = (c * X + j) * ZR

        def body(i, _):
            here = cols(i, fstep)
            g = g_ref[:, pl.ds(pl.multiple_of(x * mine + i * fstep, fstep), fstep)].astype(F32)
            n = xbuf[c, j, :, :, here].reshape(ZR, fstep).astype(F32) * r * g
            n = n.astype(BF16).astype(F32)
            sqt[here, first:first + ZR] = (n * n).T.astype(BF16)
            return 0

        lax.fori_loop(0, mine // fstep, body, 0)

    def own_squares(c):
        xbuf[c, 0] = recv[c, :, :, cols(x, mine)]
        squares(c, 0)

    def other_squares(c):
        for j in range(1, X):
            if c == 0:
                arrived(rx.at[j], rx_rs.at[j])
                for k in range(Z):
                    put_column(rx.at[j, k], j, k)
            arrived(xbuf.at[c, j], x_rs.at[c * X + j])
            squares(c, j)

    for c in range(C):
        recv[c, 0] = h_ref[pl.ds(c * tc, tc), cols(z, FS)]
    put_column(rz.at[0], 0, 0)
    for k in range(1, Z):
        arrived(rz.at[k], r_rs.at[k])
        put_column(rz.at[k], 0, k)
    for j in range(1, X):
        send(rz, rx.at[j], rx_ss.at[j], rx_rs.at[j], xdev(j))
    for c in range(C):
        for k in far_first(Z):
            arrived(recv.at[c, k], h_rs.at[c * Z + k])
        for j in range(1, X):
            send(recv.at[c, :, :, cols(flip(x, j), mine)], xbuf.at[c, j],
                 x_ss.at[c * X + j], x_rs.at[c * X + j], xdev(j))
        partial(c)
        if c < C - 1:
            own_squares(c)
            if c:
                other_squares(c - 1)

    def give_partials(i):
        for k in far_first(Z):
            send(ps.at[i, k], rs.at[i, k], p_ss.at[i * Z + k], p_rs.at[i * Z + k], zdev(k))

    def residual(i):
        here = slice(i * HB, (i + 1) * HB)
        v = own[:, here]
        for k in range(1, Z):
            arrived(rs.at[i, k], p_rs.at[i * Z + k])
            v = v + rs[i, k].astype(F32)
        d = (v * scale - t_ref[:, here].astype(F32)).astype(BF16)
        dall[i, :, 0, 0] = d.reshape(C, tc, HB)
        for k in far_first(Z):
            send(dall.at[i, :, 0, 0], dall.at[i, :, 0, k], d_ss.at[i * Z + k], d_rs.at[i * Z + k],
                 zdev(k))
        forward(i, 0)

    def forward(i, k):
        for j in range(1, X):
            s = (i * X + j) * Z + k
            send(dall.at[i, :, 0, k], dall.at[i, :, j, k], e_ss.at[s], e_rs.at[s], xdev(j))

    def residuals_on(i):
        for k in far_first(Z):
            arrived(dall.at[i, :, 0, k], d_rs.at[i * Z + k])
            forward(i, k)

    def fisher_rows(i, q):
        d = dall[i].reshape(tokens, HB).astype(F32)
        return jnp.dot(sqt[cols(q, Q), :], (d * d).astype(BF16), preferred_element_type=F32)

    def fisher(i):
        for j in range(1, X):
            for k in range(Z):
                s = (i * X + j) * Z + k
                arrived(dall.at[i, :, j, k], e_rs.at[s])
        for k in far_first(T):
            f = fisher_rows(i, flip(m, k))
            if k == 1:
                f1send[i] = f
                send(f1send.at[i], f1recv.at[i], f_ss.at[i * T + k], f_rs.at[i * T + k], tdev(k))
            else:
                fsend[i, k] = f.astype(BF16)
                send(fsend.at[i, k], frecv.at[i, k], f_ss.at[i * T + k], f_rs.at[i * T + k],
                     tdev(k))

    def block(j, i):
        return o_ref.at[cols(flip(m, j), Q), pl.ds(i * HB, HB)]

    def share(j, b, i):
        s = i * T + (j ^ b)
        send(block(j, i), block(j, i), o_ss.at[s], o_rs.at[s], tdev(b))

    def merge(i):
        here = slice(i * HB, (i + 1) * HB)
        den = fisher_rows(i, m)
        num = den * w_ref[cols(x * T + m, Q), here].astype(F32)
        for k in range(1, T):
            if i == 0:
                arrived(wq.at[k], w_rs.at[k])
            if k == 1:
                arrived(f1recv.at[i], f_rs.at[i * T + k])
                f = f1recv[i]
            else:
                arrived(frecv.at[i, k], f_rs.at[i * T + k])
                f = frecv[i, k].astype(F32)
            den = den + f
            num = num + f * wq[k, :, here].astype(F32)
        o_ref[cols(m, Q), here] = num / den
        share(0, T // 2, i)

    def share_on(i):
        held, b = [0], T // 2
        while b > 1:
            for j in held:
                arrived(block(j ^ b, i), o_rs.at[i * T + (j ^ b)])
                share(j, b // 2, i)
                share(j ^ b, b // 2, i)
            held = held + [j ^ b for j in held]
            b //= 2

    def back(c, j, total):
        d = jnp.concatenate([dall[i, c, j].reshape(ZR, HB) for i in range(B)], axis=1)
        b = lax.dot_general(d, w_ref[cols(x, mine), :], (((1,), (1,)), ((), ())),
                            preferred_element_type=F32) * scale
        r = rcol[c, j].reshape(ZR, 128)[:, 0:1]
        b = b * (xbuf[c, j].reshape(ZR, mine).astype(F32) * r)
        return total + jnp.sum(b * b, axis=0, keepdims=True)

    give_partials(0)
    if B > 1:
        give_partials(1)
    own_squares(C - 1)
    if C > 1:
        other_squares(C - 2)
    for t in range(B + 4):
        if t < B:
            residual(t)
        if t + 2 < B:
            give_partials(t + 2)
        if t == 0:
            other_squares(C - 1)
        if 0 <= t - 1 < B:
            residuals_on(t - 1)
        if 0 <= t - 2 < B:
            fisher(t - 2)
        if 0 <= t - 3 < B:
            if t - 3 == B - 1:
                gfish = jnp.zeros((1, mine), F32)
                for c in range(C):
                    for j in range(X):
                        gfish = back(c, j, gfish)
                gbuf[0, 0:1, :] = gfish * g_ref[:, cols(x, mine)].astype(F32)
                gbuf[0, 1:2, :] = gfish
                gbuf[0, 2:8, :] = jnp.zeros((6, mine), F32)
                for k in range(1, T):
                    send(gbuf.at[0], gbuf.at[k], g_ss.at[k], g_rs.at[k], tdev(k))
            merge(t - 3)
        if 0 <= t - 4 < B:
            share_on(t - 4)

    for k in range(1, T):
        arrived(gbuf.at[k], g_rs.at[k])
    sums = [gbuf[k] for k in range(T)]
    while len(sums) > 1:
        sums = [sums[i] + sums[i + 1] for i in range(0, len(sums), 2)]
    og_ref[...] = sums[0][0:1, :] / sums[0][1:2, :]
    for i in range(B):
        for j in range(0, T, 2):
            arrived(block(j ^ 1, i), o_rs.at[i * T + (j ^ 1)])
    for c in pending:
        c.wait_send()


def body(T, Z, X, hidden, target, weight, gain):
    _, tb, D = hidden.shape
    _, FS, H = weight.shape
    mine = FS // X
    Q = mine // T
    S = X * Z
    C = 2
    B = H // 128
    tc = tb // C
    dma = lambda n: pltpu.SemaphoreType.DMA((n,))
    vmem = pltpu.VMEM
    flops = 2 * S * tb * mine * H * 3
    merged, merged_gain = pl.pallas_call(
        functools.partial(kernel, T, Z, X, C, B),
        out_shape=(jax.ShapeDtypeStruct((mine, H), F32), jax.ShapeDtypeStruct((1, mine), F32)),
        in_specs=[pl.BlockSpec(memory_space=pltpu.VMEM)] * 4,
        out_specs=[pl.BlockSpec(memory_space=pltpu.VMEM)] * 2,
        scratch_shapes=[
            vmem((C, Z, tc, FS), BF16),
            vmem((C, X, Z, tc, mine), BF16),
            vmem((Z, 8, 128), F32),
            vmem((X, Z, 8, 128), F32),
            vmem((C, X, Z, tc, 128), F32),
            vmem((tb, H), F32),
            vmem((B, Z, tb, H // B), BF16),
            vmem((B, Z, tb, H // B), BF16),
            vmem((B, C, X, Z, tc, H // B), BF16),
            vmem((mine, S * tb), BF16),
            vmem((B, T, Q, H // B), BF16),
            vmem((B, T, Q, H // B), BF16),
            vmem((B, Q, H // B), F32),
            vmem((B, Q, H // B), F32),
            vmem((T, Q, H), BF16),
            vmem((T, 8, mine), F32),
            dma(C * Z), dma(C * Z), dma(Z), dma(Z), dma(C * X), dma(C * X), dma(X), dma(X),
            dma(B * Z), dma(B * Z), dma(B * Z), dma(B * Z), dma(B * S), dma(B * S),
            dma(T), dma(T), dma(B * T), dma(B * T), dma(T), dma(T), dma(B * T), dma(B * T),
        ],
        cost_estimate=pl.CostEstimate(flops=flops, bytes_accessed=8 << 20, transcendentals=0),
        compiler_params=pltpu.CompilerParams(
            collective_id=0, has_side_effects=True, vmem_limit_bytes=56 << 20),
    )(hidden[0], target[0], weight[0], gain)
    return merged, merged_gain[0]


def solution(mesh):
    T, Z, X = (mesh.shape[a] for a in ("template", "fsdp", "dp"))
    in_specs = (
        P("template", ("fsdp", "dp"), None),
        P("template", ("fsdp", "dp"), None),
        P("template", "fsdp", None),
        P("template", "fsdp"),
    )
    out_specs = (P(("fsdp", "dp"), None), P(("fsdp", "dp")))
    return jax.shard_map(functools.partial(body, T, Z, X), mesh=mesh, in_specs=in_specs,
                         out_specs=out_specs, check_vma=False)
```

time: 120 us -> 121 us (level)
  the two profiles are of different devices: /device:TPU:25 before, /device:TPU:1 now
where the time goes in v3:
time: 121 us; the launch traced here: 120 us
  Pallas kernels  116 us (96%)
  local copies, waits for them, and re-layouts  3.68 us (3%)
    pallas_call x1, Pallas kernels, body(): pl.pallas_call(functools.partial(kernel, T, Z, X, C, B), out_shape=(jax.S...  116 us
    unnamed x4, local copies, waits for them, and re-layouts  3.68 us

profile of v3, /device:TPU:1, one launch (start us, length us, event | category | flops | bytes accessed | tf_op | source)
XLA Modules:
  0.0 120.3 jit_solution(18112845389737430281)
XLA Ops:
  0.6 116.0 %shard_map.59 = (f32[1024,512]{1,0:T(8,128)}, f32[1,1024]{1,0:T(1,128)}) custom-call(bf16[128,8192]{1,0:T(8,128)(2,1)} %bitcast.5, bf16[128,512]{1,0:T(8,128)(2,1)} %bitcast.7, bf16[2048,512]{1,0:T(8,128)(2,1)} %bitcast.6, bf16[1,2048]{1,0:T(2,128)(2,1)} %g_ref.1), custom_call_target="tpu_custom_call" | custom-call | flops 3221225472 | bytes 8388608 | tf_op jit(solution)/shard_map/pallas_call | solution.py:314
  116.6 0.0 copy-start
  116.7 3.1 %copy.8 = f32[1024,512]{1,0:T(8,128)} copy(f32[1024,512]{1,0:T(8,128)} %get-tuple-element.8) | data formatting | bytes 4194304
  119.7 0.0 copy-done
  119.7 0.6 copy.9
Async XLA Ops:
  116.6 3.1 %copy-start = (f32[1,1024]{1,0:T(1,128)S(1)}, f32[1,1024]{1,0:T(1,128)}, u32[]{:S(2)}) copy-start(f32[1,1024]{1,0:T(1,128)} %get-tuple-element.5) | copy-start | bytes 12292

commit v4 on v3

--- a/solution.py
+++ b/solution.py
@@ -27,7 +27,7 @@
 
 
 def kernel(T, Z, X, C, B, h_ref, t_ref, w_ref, g_ref, o_ref, og_ref,
-           recv, xbuf, rz, rx, rcol, own, ps, rs, dall, sqt, fsend, frecv,
+           recv, xbuf, turned, rz, rx, rcol, own, ps, rs, dall, sqt, fsend, frecv,
            f1send, f1recv, wq, gbuf,
            h_ss, h_rs, r_ss, r_rs, x_ss, x_rs, rx_ss, rx_rs, p_ss, p_rs,
            d_ss, d_rs, e_ss, e_rs, w_ss, w_rs, f_ss, f_rs, g_ss, g_rs, o_ss, o_rs):
@@ -71,10 +71,12 @@
         pl.semaphore_signal(barrier, inc=1, device_id=dev, device_id_type=MESH)
     pl.semaphore_wait(barrier, len(peers))
 
-    for c in range(C):
+    def send_hidden(c):
         for k in far_first(Z):
             send(h_ref.at[pl.ds(c * tc, tc), cols(flip(z, k), FS)], recv.at[c, k],
                  h_ss.at[c * Z + k], h_rs.at[c * Z + k], zdev(k))
+
+    send_hidden(0)
 
     step = min(512, D)
 
@@ -90,6 +92,8 @@
     rz[0] = jnp.broadcast_to(ratio, (tb, 128)).T[0:8, :]
     for k in far_first(Z):
         send(rz.at[0], rz.at[k], r_ss.at[k], r_rs.at[k], zdev(k))
+    for c in range(1, min(C, 2)):
+        send_hidden(c)
     for k in range(1, T):
         send(w_ref.at[cols(x * T + flip(m, k), Q)], wq.at[k], w_ss.at[k], w_rs.at[k], tdev(k))
 
@@ -147,6 +151,7 @@
 
     for c in range(C):
         recv[c, 0] = h_ref[pl.ds(c * tc, tc), cols(z, FS)]
+    turned[...] = w_ref[cols(x, mine), :].T
     put_column(rz.at[0], 0, 0)
     for k in range(1, Z):
         arrived(rz.at[k], r_rs.at[k])
@@ -156,6 +161,8 @@
     for c in range(C):
         for k in far_first(Z):
             arrived(recv.at[c, k], h_rs.at[c * Z + k])
+        if c + 2 < C:
+            send_hidden(c + 2)
         for j in range(1, X):
             send(recv.at[c, :, :, cols(flip(x, j), mine)], xbuf.at[c, j],
                  x_ss.at[c * X + j], x_rs.at[c * X + j], xdev(j))
@@ -248,8 +255,7 @@
 
     def back(c, j, total):
         d = jnp.concatenate([dall[i, c, j].reshape(ZR, HB) for i in range(B)], axis=1)
-        b = lax.dot_general(d, w_ref[cols(x, mine), :], (((1,), (1,)), ((), ())),
-                            preferred_element_type=F32) * scale
+        b = jnp.dot(d, turned[...], preferred_element_type=F32) * scale
         r = rcol[c, j].reshape(ZR, 128)[:, 0:1]
         b = b * (xbuf[c, j].reshape(ZR, mine).astype(F32) * r)
         return total + jnp.sum(b * b, axis=0, keepdims=True)
@@ -258,17 +264,17 @@
     if B > 1:
         give_partials(1)
     own_squares(C - 1)
-    if C > 1:
-        other_squares(C - 2)
     for t in range(B + 4):
         if t < B:
             residual(t)
         if t + 2 < B:
             give_partials(t + 2)
-        if t == 0:
-            other_squares(C - 1)
+        if t == 0 and C > 1:
+            other_squares(C - 2)
         if 0 <= t - 1 < B:
             residuals_on(t - 1)
+        if t == 1:
+            other_squares(C - 1)
         if 0 <= t - 2 < B:
             fisher(t - 2)
         if 0 <= t - 3 < B:
@@ -299,13 +305,17 @@
         c.wait_send()
 
 
+def hand_on(i_ref, o_ref):
+    o_ref[...] = i_ref[...]
+
+
 def body(T, Z, X, hidden, target, weight, gain):
     _, tb, D = hidden.shape
     _, FS, H = weight.shape
     mine = FS // X
     Q = mine // T
     S = X * Z
-    C = 2
+    C = 4
     B = H // 128
     tc = tb // C
     dma = lambda n: pltpu.SemaphoreType.DMA((n,))
@@ -319,6 +329,7 @@
         scratch_shapes=[
             vmem((C, Z, tc, FS), BF16),
             vmem((C, X, Z, tc, mine), BF16),
+            vmem((H, mine), BF16),
             vmem((Z, 8, 128), F32),
             vmem((X, Z, 8, 128), F32),
             vmem((C, X, Z, tc, 128), F32),
@@ -341,6 +352,14 @@
         compiler_params=pltpu.CompilerParams(
             collective_id=0, has_side_effects=True, vmem_limit_bytes=56 << 20),
     )(hidden[0], target[0], weight[0], gain)
+    rows = mine // 4
+    merged = pl.pallas_call(
+        hand_on,
+        out_shape=jax.ShapeDtypeStruct((mine, H), F32),
+        grid=(4,),
+        in_specs=[pl.BlockSpec((rows, H), lambda i: (i, 0))],
+        out_specs=pl.BlockSpec((rows, H), lambda i: (i, 0)),
+    )(merged)
     return merged, merged_gain[0]
 
 

time: 121 us -> 109 us (0.901)
  Pallas kernels: 116 us -> 107 us
  local copies, waits for them, and re-layouts: 3.68 us -> 0.6 us
    pallas_call x1, Pallas kernels: 116 us -> 103 us  [body(): pl.pallas_call(functools.partial(kernel, T, Z, X, C, B), out_shape=(jax.S...]
    pallas_call x0 -> x1, Pallas kernels: none -> 3.78 us  [body(): pl.pallas_call(hand_on, out_shape=jax.ShapeDtypeStruct((mine, H), F32), g...]
    unnamed x4 -> x3, local copies, waits for them, and re-layouts: 3.68 us -> 0.6 us
where the time goes in v4:
time: 109 us; the launch traced here: 108 us
  Pallas kernels  107 us (98%)
    pallas_call x1, Pallas kernels, body(): pl.pallas_call(functools.partial(kernel, T, Z, X, C, B), out_shape=(jax.S...  103 us
    pallas_call x1, Pallas kernels, body(): pl.pallas_call(hand_on, out_shape=jax.ShapeDtypeStruct((mine, H), F32), g...  3.78 us

profile of v4, /device:TPU:1, one launch (start us, length us, event | category | flops | bytes accessed | tf_op | source)
XLA Modules:
  0.0 108.4 jit_solution(7878168274267125253)
XLA Ops:
  0.6 103.4 %shard_map.59 = (f32[1024,512]{1,0:T(8,128)}, f32[1,1024]{1,0:T(1,128)}) custom-call(bf16[128,8192]{1,0:T(8,128)(2,1)} %bitcast.5, bf16[128,512]{1,0:T(8,128)(2,1)} %bitcast.7, bf16[2048,512]{1,0:T(8,128)(2,1)} %bitcast.6, bf16[1,2048]{1,0:T(2,128)(2,1)} %g_ref.1), custom_call_target="tpu_custom_call" | custom-call | flops 3221225472 | bytes 8388608 | tf_op jit(solution)/shard_map/pallas_call | solution.py:324
  104.0 0.0 copy-start
  104.0 3.8 %shard_map.60 = f32[1024,512]{1,0:T(8,128)} custom-call(f32[1024,512]{1,0:T(8,128)} %get-tuple-element.4.i_ref), custom_call_target="tpu_custom_call" | custom-call | tf_op jit(solution)/shard_map/pallas_call | solution.py:356
  107.8 0.0 copy-done
  107.8 0.6 copy.7
Async XLA Ops:
  104.0 3.8 %copy-start = (f32[1,1024]{1,0:T(1,128)S(1)}, f32[1,1024]{1,0:T(1,128)}, u32[]{:S(2)}) copy-start(f32[1,1024]{1,0:T(1,128)} %get-tuple-element.5) | copy-start | bytes 12292

commit v5 on v4

--- a/solution.py
+++ b/solution.py
@@ -27,7 +27,7 @@
 
 
 def kernel(T, Z, X, C, B, h_ref, t_ref, w_ref, g_ref, o_ref, og_ref,
-           recv, xbuf, turned, rz, rx, rcol, own, ps, rs, dall, sqt, fsend, frecv,
+           recv, xbuf, turned, rz, rx, rcol, pacc, ps, rs, dall, sqt, fsend, frecv,
            f1send, f1recv, wq, gbuf,
            h_ss, h_rs, r_ss, r_rs, x_ss, x_rs, rx_ss, rx_rs, p_ss, p_rs,
            d_ss, d_rs, e_ss, e_rs, w_ss, w_rs, f_ss, f_rs, g_ss, g_rs, o_ss, o_rs):
@@ -114,11 +114,28 @@
             return total + jnp.dot(n, w_ref[here, :], preferred_element_type=F32)
 
         v = lax.fori_loop(0, FS // wstep, body, jnp.zeros((ZR, H), F32))
-        own[pl.ds(c * tc, tc), :] = v[0:tc, :]
-        for i in range(B):
-            for k in range(1, Z):
-                ps[i, k, pl.ds(c * tc, tc), :] = (
-                    v[k * tc:(k + 1) * tc, i * HB:(i + 1) * HB].astype(BF16))
+        pacc[c] = v.reshape(Z, tc, H)
+
+    steps = Z.bit_length() - 1
+
+    def sum_send(c, n):
+        b = 1 << n
+        for k in range(b, Z, 2 * b):
+            ps[c, k] = pacc[c, k].astype(BF16)
+            send(ps.at[c, k], rs.at[c, k], p_ss.at[c * Z + k], p_rs.at[c * Z + k], zdev(b))
+
+    def sum_take(c, n):
+        b = 1 << n
+        for k in range(b, Z, 2 * b):
+            arrived(rs.at[c, k], p_rs.at[c * Z + k])
+            pacc[c, k - b] += rs[c, k].astype(F32)
+
+    def sum_on(t):
+        for n in range(1, steps + 1):
+            if 0 <= t - n < C:
+                sum_take(t - n, n - 1)
+                if n < steps:
+                    sum_send(t - n, n)
 
     fstep = min(256, mine)
 
@@ -167,21 +184,16 @@
             send(recv.at[c, :, :, cols(flip(x, j), mine)], xbuf.at[c, j],
                  x_ss.at[c * X + j], x_rs.at[c * X + j], xdev(j))
         partial(c)
+        sum_send(c, 0)
+        sum_on(c)
+        own_squares(c)
         if c < C - 1:
-            own_squares(c)
             if c:
                 other_squares(c - 1)
 
-    def give_partials(i):
-        for k in far_first(Z):
-            send(ps.at[i, k], rs.at[i, k], p_ss.at[i * Z + k], p_rs.at[i * Z + k], zdev(k))
-
     def residual(i):
         here = slice(i * HB, (i + 1) * HB)
-        v = own[:, here]
-        for k in range(1, Z):
-            arrived(rs.at[i, k], p_rs.at[i * Z + k])
-            v = v + rs[i, k].astype(F32)
+        v = pacc[:, 0, :, here].reshape(tb, HB)
         d = (v * scale - t_ref[:, here].astype(F32)).astype(BF16)
         dall[i, :, 0, 0] = d.reshape(C, tc, HB)
         for k in far_first(Z):
@@ -260,25 +272,22 @@
         b = b * (xbuf[c, j].reshape(ZR, mine).astype(F32) * r)
         return total + jnp.sum(b * b, axis=0, keepdims=True)
 
-    give_partials(0)
-    if B > 1:
-        give_partials(1)
-    own_squares(C - 1)
-    for t in range(B + 4):
+    sum_on(C)
+    if C > 1:
+        other_squares(C - 2)
+    for t in range(C + 1, C + steps):
+        sum_on(t)
+    for i in range(B):
+        residual(i)
+    for t in range(B + 3):
         if t < B:
-            residual(t)
-        if t + 2 < B:
-            give_partials(t + 2)
-        if t == 0 and C > 1:
-            other_squares(C - 2)
+            residuals_on(t)
+        if t == 0:
+            other_squares(C - 1)
         if 0 <= t - 1 < B:
-            residuals_on(t - 1)
-        if t == 1:
-            other_squares(C - 1)
+            fisher(t - 1)
         if 0 <= t - 2 < B:
-            fisher(t - 2)
-        if 0 <= t - 3 < B:
-            if t - 3 == B - 1:
+            if t - 2 == B - 1:
                 gfish = jnp.zeros((1, mine), F32)
                 for c in range(C):
                     for j in range(X):
@@ -288,9 +297,9 @@
                 gbuf[0, 2:8, :] = jnp.zeros((6, mine), F32)
                 for k in range(1, T):
                     send(gbuf.at[0], gbuf.at[k], g_ss.at[k], g_rs.at[k], tdev(k))
-            merge(t - 3)
-        if 0 <= t - 4 < B:
-            share_on(t - 4)
+            merge(t - 2)
+        if 0 <= t - 3 < B:
+            share_on(t - 3)
 
     for k in range(1, T):
         arrived(gbuf.at[k], g_rs.at[k])
@@ -305,8 +314,14 @@
         c.wait_send()
 
 
-def hand_on(i_ref, o_ref):
-    o_ref[...] = i_ref[...]
+def hand_on(i_ref, o_ref, sems):
+    rows = i_ref.shape[0] // 4
+    copies = [pltpu.make_async_copy(i_ref.at[pl.ds(i * rows, rows)], o_ref.at[pl.ds(i * rows, rows)],
+                                    sems.at[i]) for i in range(4)]
+    for c in copies:
+        c.start()
+    for c in copies:
+        c.wait()
 
 
 def body(T, Z, X, hidden, target, weight, gain):
@@ -333,9 +348,9 @@
             vmem((Z, 8, 128), F32),
             vmem((X, Z, 8, 128), F32),
             vmem((C, X, Z, tc, 128), F32),
-            vmem((tb, H), F32),
-            vmem((B, Z, tb, H // B), BF16),
-            vmem((B, Z, tb, H // B), BF16),
+            vmem((C, Z, tc, H), F32),
+            vmem((C, Z, tc, H), BF16),
+            vmem((C, Z, tc, H), BF16),
             vmem((B, C, X, Z, tc, H // B), BF16),
             vmem((mine, S * tb), BF16),
             vmem((B, T, Q, H // B), BF16),
@@ -345,20 +360,19 @@
             vmem((T, Q, H), BF16),
             vmem((T, 8, mine), F32),
             dma(C * Z), dma(C * Z), dma(Z), dma(Z), dma(C * X), dma(C * X), dma(X), dma(X),
-            dma(B * Z), dma(B * Z), dma(B * Z), dma(B * Z), dma(B * S), dma(B * S),
+            dma(C * Z), dma(C * Z), dma(B * Z), dma(B * Z), dma(B * S), dma(B * S),
             dma(T), dma(T), dma(B * T), dma(B * T), dma(T), dma(T), dma(B * T), dma(B * T),
         ],
         cost_estimate=pl.CostEstimate(flops=flops, bytes_accessed=8 << 20, transcendentals=0),
         compiler_params=pltpu.CompilerParams(
             collective_id=0, has_side_effects=True, vmem_limit_bytes=56 << 20),
     )(hidden[0], target[0], weight[0], gain)
-    rows = mine // 4
     merged = pl.pallas_call(
         hand_on,
         out_shape=jax.ShapeDtypeStruct((mine, H), F32),
-        grid=(4,),
-        in_specs=[pl.BlockSpec((rows, H), lambda i: (i, 0))],
-        out_specs=pl.BlockSpec((rows, H), lambda i: (i, 0)),
+        in_specs=[pl.BlockSpec(memory_space=pl.ANY)],
+        out_specs=pl.BlockSpec(memory_space=pl.ANY),
+        scratch_shapes=[dma(4)],
     )(merged)
     return merged, merged_gain[0]
 

time: 109 us -> 172 us (1.58)
  Pallas kernels: 107 us -> 171 us
    pallas_call x1, Pallas kernels: 3.78 us -> 64.7 us  [body(): pl.pallas_call(hand_on, out_shape=jax.ShapeDtypeStruct((mine, H), F32), i...]
    pallas_call x1, Pallas kernels: 103 us -> 106 us  [body(): pl.pallas_call(functools.partial(kernel, T, Z, X, C, B), out_shape=(jax.S...]
where the time goes in v5:
time: 172 us
  Pallas kernels  171 us (99%)
    pallas_call x1, Pallas kernels, body(): pl.pallas_call(functools.partial(kernel, T, Z, X, C, B), out_shape=(jax.S...  106 us
    pallas_call x1, Pallas kernels, body(): pl.pallas_call(hand_on, out_shape=jax.ShapeDtypeStruct((mine, H), F32), i...  64.7 us

profile of v5, /device:TPU:1, one launch (start us, length us, event | category | flops | bytes accessed | tf_op | source)
XLA Modules:
  0.0 172.0 jit_solution(11357564991646132526)
XLA Ops:
  0.6 106.0 %shard_map.59 = (f32[1024,512]{1,0:T(8,128)}, f32[1,1024]{1,0:T(1,128)}) custom-call(bf16[128,8192]{1,0:T(8,128)(2,1)} %bitcast.5, bf16[128,512]{1,0:T(8,128)(2,1)} %bitcast.7, bf16[2048,512]{1,0:T(8,128)(2,1)} %bitcast.6, bf16[1,2048]{1,0:T(2,128)(2,1)} %g_ref.1), custom_call_target="tpu_custom_call" | custom-call | flops 3221225472 | bytes 8388608 | tf_op jit(solution)/shard_map/pallas_call | solution.py:339
  106.7 0.0 copy-start
  106.7 64.7 %shard_map.60 = f32[1024,512]{1,0:T(8,128)} custom-call(f32[1024,512]{1,0:T(8,128)} %get-tuple-element.4.i_ref), custom_call_target="tpu_custom_call" | custom-call | tf_op jit(solution)/shard_map/pallas_call | solution.py:370
  171.4 0.0 copy-done
  171.4 0.6 copy.7
Async XLA Ops:
  106.7 64.7 %copy-start = (f32[1,1024]{1,0:T(1,128)S(1)}, f32[1,1024]{1,0:T(1,128)}, u32[]{:S(2)}) copy-start(f32[1,1024]{1,0:T(1,128)} %get-tuple-element.5) | copy-start | bytes 12292

commit v6 on v4

--- a/solution.py
+++ b/solution.py
@@ -214,7 +214,7 @@
                 f1send[i] = f
                 send(f1send.at[i], f1recv.at[i], f_ss.at[i * T + k], f_rs.at[i * T + k], tdev(k))
             else:
-                fsend[i, k] = f.astype(BF16)
+                fsend[i, k] = (f * f).astype(BF16)
                 send(fsend.at[i, k], frecv.at[i, k], f_ss.at[i * T + k], f_rs.at[i * T + k],
                      tdev(k))
 
@@ -237,10 +237,13 @@
                 f = f1recv[i]
             else:
                 arrived(frecv.at[i, k], f_rs.at[i * T + k])
-                f = frecv[i, k].astype(F32)
+                f = jnp.sqrt(frecv[i, k].astype(F32))
             den = den + f
             num = num + f * wq[k, :, here].astype(F32)
-        o_ref[cols(m, Q), here] = num / den
+        v = num / den
+        v2 = v * v
+        v4 = v2 * v2
+        o_ref[cols(m, Q), here] = jnp.where(v < 0, -v4, v4).astype(BF16)
         share(0, T // 2, i)
 
     def share_on(i):
@@ -305,10 +308,6 @@
         c.wait_send()
 
 
-def hand_on(i_ref, o_ref):
-    o_ref[...] = i_ref[...]
-
-
 def body(T, Z, X, hidden, target, weight, gain):
     _, tb, D = hidden.shape
     _, FS, H = weight.shape
@@ -323,7 +322,7 @@
     flops = 2 * S * tb * mine * H * 3
     merged, merged_gain = pl.pallas_call(
         functools.partial(kernel, T, Z, X, C, B),
-        out_shape=(jax.ShapeDtypeStruct((mine, H), F32), jax.ShapeDtypeStruct((1, mine), F32)),
+        out_shape=(jax.ShapeDtypeStruct((mine, H), BF16), jax.ShapeDtypeStruct((1, mine), F32)),
         in_specs=[pl.BlockSpec(memory_space=pltpu.VMEM)] * 4,
         out_specs=[pl.BlockSpec(memory_space=pltpu.VMEM)] * 2,
         scratch_shapes=[
@@ -352,15 +351,9 @@
         compiler_params=pltpu.CompilerParams(
             collective_id=0, has_side_effects=True, vmem_limit_bytes=56 << 20),
     )(hidden[0], target[0], weight[0], gain)
-    rows = mine // 4
-    merged = pl.pallas_call(
-        hand_on,
-        out_shape=jax.ShapeDtypeStruct((mine, H), F32),
-        grid=(4,),
-        in_specs=[pl.BlockSpec((rows, H), lambda i: (i, 0))],
-        out_specs=pl.BlockSpec((rows, H), lambda i: (i, 0)),
-    )(merged)
-    return merged, merged_gain[0]
+    y = merged.astype(F32)
+    r = jnp.sqrt(jnp.sqrt(jnp.abs(y)))
+    return jnp.where(y < 0, -r, r), merged_gain[0]
 
 
 def solution(mesh):

time: 109 us -> 102 us (0.936)
  Pallas kernels: 107 us -> 97.2 us
  other arithmetic: 0 us -> 3.83 us
    pallas_call x1, Pallas kernels: 103 us -> 97.2 us  [body(): pl.pallas_call(functools.partial(kernel, T, Z, X, C, B), out_shape=(jax.S...]
    select_n x0 -> x1, other arithmetic: none -> 3.83 us  [body(): return (jnp.where(y < 0, -r, r), merged_gain[0])]
    pallas_call x1 -> x0, Pallas kernels: 3.78 us -> none  [body(): pl.pallas_call(hand_on, out_shape=jax.ShapeDtypeStruct((mine, H), F32), g...]
where the time goes in v6:
time: 102 us
  Pallas kernels  97.2 us (95%)
  other arithmetic  3.83 us (4%)
    pallas_call x1, Pallas kernels, body(): pl.pallas_call(functools.partial(kernel, T, Z, X, C, B), out_shape=(jax.S...  97.2 us
    select_n x1, other arithmetic, body(): return (jnp.where(y < 0, -r, r), merged_gain[0])  3.83 us

profile of v6, /device:TPU:1, one launch (start us, length us, event | category | flops | bytes accessed | tf_op | source)
XLA Modules:
  0.0 102.3 jit_solution(7137046488791963845)
XLA Ops:
  0.6 97.2 %shard_map.59 = (bf16[1024,512]{1,0:T(8,128)(2,1)}, f32[1,1024]{1,0:T(1,128)}) custom-call(bf16[128,8192]{1,0:T(8,128)(2,1)} %bitcast.5, bf16[128,512]{1,0:T(8,128)(2,1)} %bitcast.7, bf16[2048,512]{1,0:T(8,128)(2,1)} %bitcast.6, bf16[1,2048]{1,0:T(2,128)(2,1)} %g_ref.1), custom_call_target="tpu_custom_call" | custom-call | flops 3221225472 | bytes 8388608 | tf_op jit(solution)/shard_map/pallas_call | solution.py:323
  97.8 0.0 copy-start
  97.8 3.8 %negate_select_fusion = f32[1024,512]{1,0:T(8,128)} fusion(bf16[1024,512]{1,0:T(8,128)(2,1)} %get-tuple-element.4), kind=kLoop, calls=%fused_computation | loop fusion | flops 2621440 | bytes 3145728 | tf_op jit(solution)/shard_map/jit(_where)/select_n | solution.py:356
  101.7 0.0 copy-done
  101.7 0.6 copy.7
Async XLA Ops:
  97.8 3.8 %copy-start = (f32[1,1024]{1,0:T(1,128)S(1)}, f32[1,1024]{1,0:T(1,128)}, u32[]{:S(2)}) copy-start(f32[1,1024]{1,0:T(1,128)} %get-tuple-element.5) | copy-start | bytes 12292

commit v7 on v6

--- a/solution.py
+++ b/solution.py
@@ -315,7 +315,7 @@
     Q = mine // T
     S = X * Z
     C = 4
-    B = H // 128
+    B = H // 256
     tc = tb // C
     dma = lambda n: pltpu.SemaphoreType.DMA((n,))
     vmem = pltpu.VMEM

time: 102 us -> 107 us (1.049); the launches traced: 102 us -> 105 us
  Pallas kernels: 97.2 us -> 100 us
    pallas_call x1, Pallas kernels: 97.2 us -> 100 us  [body(): pl.pallas_call(functools.partial(kernel, T, Z, X, C, B), out_shape=(jax.S...]
where the time goes in v7:
time: 107 us; the launch traced here: 105 us
  Pallas kernels  100 us (93%)
  other arithmetic  3.83 us (4%)
    pallas_call x1, Pallas kernels, body(): pl.pallas_call(functools.partial(kernel, T, Z, X, C, B), out_shape=(jax.S...  100 us
    select_n x1, other arithmetic, body(): return (jnp.where(y < 0, -r, r), merged_gain[0])  3.83 us

profile of v7, /device:TPU:1, one launch (start us, length us, event | category | flops | bytes accessed | tf_op | source)
XLA Modules:
  0.0 105.5 jit_solution(14555351515067335011)
XLA Ops:
  0.6 100.4 %shard_map.59 = (bf16[1024,512]{1,0:T(8,128)(2,1)}, f32[1,1024]{1,0:T(1,128)}) custom-call(bf16[128,8192]{1,0:T(8,128)(2,1)} %bitcast.5, bf16[128,512]{1,0:T(8,128)(2,1)} %bitcast.7, bf16[2048,512]{1,0:T(8,128)(2,1)} %bitcast.6, bf16[1,2048]{1,0:T(2,128)(2,1)} %g_ref.1), custom_call_target="tpu_custom_call" | custom-call | flops 3221225472 | bytes 8388608 | tf_op jit(solution)/shard_map/pallas_call | solution.py:323
  101.1 0.0 copy-start
  101.1 3.8 %negate_select_fusion = f32[1024,512]{1,0:T(8,128)} fusion(bf16[1024,512]{1,0:T(8,128)(2,1)} %get-tuple-element.4), kind=kLoop, calls=%fused_computation | loop fusion | flops 2621440 | bytes 3145728 | tf_op jit(solution)/shard_map/jit(_where)/select_n | solution.py:356
  104.9 0.0 copy-done
  104.9 0.6 copy.7
Async XLA Ops:
  101.1 3.8 %copy-start = (f32[1,1024]{1,0:T(1,128)S(1)}, f32[1,1024]{1,0:T(1,128)}, u32[]{:S(2)}) copy-start(f32[1,1024]{1,0:T(1,128)} %get-tuple-element.5) | copy-start | bytes 12292
